TPU v7x, 32 devices: a whole 2x2x4 slice. The times are simulated.
32 devices in a mesh: paths: 2 (over x), node: 16 (over z, y, core).
Axes of the slice: x: 2, y: 2, z: 4, core: 2. Of those that a mesh axis runs over, the one named last changes fastest.
Arguments:
- amplitudes: float32 [2, 2097152], P(None, ('paths', 'node')), parts along dimension 1, may hold values from -6 to 6
- gates: float32 [2, 12, 128, 128], replicated, may hold values from -0.375 to 0.375
Outputs:
- final_state: float32 [2, 2097152], P(None, ('paths', 'node')), parts along dimension 1
There are 2 independent parts, one for each index of `paths`. A program takes and returns all parts, laid end to end along the dimension named above; an argument that names none is the same for every part. Nothing has to cross between parts.
All inputs are finite; a program needn't handle non-finite values.
Results may differ from a plain program's by a relative error of at most 0.0001.
Values sent between devices are 32-bit elements; how exact they have to be, the bound alone decides.
A program may use at most 64 MiB of HBM per device.

v0:
```python
import functools

import jax
import jax.numpy as jnp
from jax import lax
from jax.experimental import pallas as pl
from jax.experimental.pallas import tpu as pltpu
from jax.sharding import PartitionSpec as P

F32 = jnp.float32
BF16 = jnp.bfloat16
ORDER = 128
LANES = 128
QUARTERS = 4


def split(x):
    high = x.astype(BF16)
    low = (x - high.astype(F32)).astype(BF16)
    return high, low


def exchange_bits(groups):
    lane = lax.broadcasted_iota(jnp.int32, groups[0].shape, 1)
    turned = [groups[0]] + [pltpu.roll(groups[i], 16 * i, 1) for i in range(1, 8)]
    turned = [turned[-i % 8] for i in range(8)]
    for k in range(3):
        here = (lane & (16 << k)) == 0
        turned = [jnp.where(here, turned[i], turned[(i - (1 << k)) % 8]) for i in range(8)]
    return [turned[0]] + [pltpu.roll(turned[i], LANES - 16 * i, 1) for i in range(1, 8)]


def swap_blocks(y):
    columns = []
    for start in range(0, y.shape[1], LANES):
        parts = []
        for base in range(0, 2 * ORDER, ORDER):
            parts += exchange_bits(
                [y[base + 16 * i : base + 16 * i + 16, start : start + LANES] for i in range(8)]
            )
        columns.append(jnp.concatenate(parts, 0))
    return jnp.concatenate(columns, 1)


def to_left(y):
    return jnp.concatenate(
        [
            jnp.concatenate([y[i : i + ORDER, :LANES], y[i : i + ORDER, LANES:]], 0)
            for i in range(0, y.shape[0], ORDER)
        ],
        1,
    )


def to_right(y):
    return jnp.concatenate(
        [
            jnp.concatenate([y[:ORDER, i : i + LANES], y[ORDER:, i : i + LANES]], 1)
            for i in range(0, y.shape[1], LANES)
        ],
        0,
    )


def prepare(g_ref, gc_ref, m, permuted):
    real_high, real_low = split(g_ref[0, m])
    imag_high, imag_low = split(g_ref[1, m])
    blocks = [real_high, real_low, imag_high, imag_low]
    if permuted:
        row = lax.broadcasted_iota(jnp.int32, (ORDER, ORDER), 0)
        column = lax.broadcasted_iota(jnp.int32, (ORDER, ORDER), 1)
        place = ((row & 15) << 3) + (row >> 4)
        move = jnp.where(column == place, 1.0, 0.0).astype(BF16)
        wide = jnp.dot(move, jnp.concatenate(blocks, 1), preferred_element_type=F32).astype(BF16)
        blocks = [
            lax.dot_general(
                wide[:, i * ORDER : (i + 1) * ORDER], move, (((1,), (1,)), ((), ())), preferred_element_type=F32
            ).astype(BF16)
            for i in range(4)
        ]
    real_high, real_low, imag_high, imag_low = blocks
    gc_ref[m, :ORDER, :] = jnp.concatenate([real_high, -imag_high, real_low, -imag_low, real_high, -imag_high], 1)
    gc_ref[m, ORDER:, :] = jnp.concatenate([imag_high, real_high, imag_low, real_low, imag_high, real_high], 1)


def prepare_halves(g_ref, gh_ref, k, m):
    real, imag = g_ref[0, m], g_ref[1, m]
    half = ORDER // 2
    below = lax.broadcasted_iota(jnp.int32, (ORDER, ORDER), 1) < half

    def fold(a, b):
        return jnp.where(below, a, pltpu.roll(b, half, 1)), jnp.where(below, pltpu.roll(a, half, 1), b)

    for part, sides in enumerate((fold(real, -imag), fold(imag, real))):
        for h in range(2):
            high, low = split(sides[h])
            gh_ref[k, h, part * ORDER : (part + 1) * ORDER, :] = jnp.concatenate([high, low, high], 1)


def left(gate, x):
    high, low = split(x)
    return jnp.dot(gate, jnp.concatenate([high, high, low], 0), preferred_element_type=F32)


def right(gate, x):
    high, low = split(x)
    return lax.dot_general(
        jnp.concatenate([high, high, low], 1), gate, (((1,), (1,)), ((), ())), preferred_element_type=F32
    )


def reversed3(x):
    return ((x & 1) << 2) | (x & 2) | ((x >> 2) & 1)


def kernel(
    nodes, distinct, x_hbm, g_hbm, o_ref, x_ref, g_ref, gc, gh, sa, sb, sc, sd, r1, r2, in_x, in_g, send1, recv1, send2, recv2
):
    rows = sa.shape[1]
    quarter = rows // QUARTERS

    def load_x(a):
        some = pl.ds(2 * a * quarter, 2 * quarter)
        return pltpu.make_async_copy(x_hbm.at[some, :], x_ref.at[some, :], in_x.at[a])

    def load_gate(m):
        return pltpu.make_async_copy(g_hbm.at[:, m], g_ref.at[:, m], in_g.at[m])

    sequence = list(dict.fromkeys(g % distinct for g in (0, 1, 4, 2, 3, 5, 8, 6, 7, 9, 10, 11)))
    load_gate(sequence[0]).start()
    for a in range(QUARTERS):
        load_x(a).start()
    for m in sequence[1:]:
        load_gate(m).start()
    me = lax.axis_index("node")
    barrier = pltpu.get_barrier_semaphore()
    for i in range(1, nodes):
        pl.semaphore_signal(barrier, inc=1, device_id={"node": me ^ i}, device_id_type=pl.DeviceIdType.MESH)

    ready = set()
    loaded = set()

    def arrive(m):
        if m not in loaded:
            loaded.add(m)
            load_gate(m).wait()

    def gate(g):
        m = g % distinct
        if m not in ready:
            ready.add(m)
            arrive(m)
            prepare(g_ref, gc, m, g % 4 == 1)
        return gc[m]

    def store(ref, first, y):
        ref[0, pl.ds(first, y.shape[0]), :] = y[:, :LANES]
        ref[1, pl.ds(first, y.shape[0]), :] = y[:, LANES:]

    def load_quarters(ref, firsts):
        return jnp.concatenate(
            [
                jnp.concatenate([ref[0, pl.ds(first, quarter), :], ref[1, pl.ds(first, quarter), :]], 0)
                for first in firsts
            ],
            1,
        )

    def store_quarters(ref, firsts, y):
        for i, first in enumerate(firsts):
            ref[0, pl.ds(first, quarter), :] = y[:ORDER, i * LANES : (i + 1) * LANES]
            ref[1, pl.ds(first, quarter), :] = y[ORDER:, i * LANES : (i + 1) * LANES]

    def strided(g, src, dst):
        matrix = gate(g)
        for pair in range(2):
            x = jnp.concatenate(
                [
                    jnp.concatenate([src[part, pl.ds(2 * pair + c, ORDER, stride=4), :] for part in range(2)], 0)
                    for c in range(2)
                ],
                1,
            )
            y = left(matrix, x)
            for c in range(2):
                for part in range(2):
                    dst[part, pl.ds(2 * pair + c, ORDER, stride=4), :] = y[
                        part * ORDER : (part + 1) * ORDER, c * LANES : (c + 1) * LANES
                    ]

    def halves_of(g, k):
        arrive(g % distinct)
        prepare_halves(g_ref, gh, k, g % distinct)

    def strided_half(k, src, dst, h, add):
        matrix = gh[k, h]
        base = pl.multiple_of(h * (rows // 2), rows // 2)
        for pair in range(2):
            x = jnp.concatenate(
                [
                    jnp.concatenate(
                        [src[part, pl.ds(base + 2 * pair + c, ORDER // 2, stride=4), :] for part in range(2)], 0
                    )
                    for c in range(2)
                ],
                1,
            )
            y = left(matrix, x)
            for c in range(2):
                for part in range(2):
                    z = y[part * ORDER : (part + 1) * ORDER, c * LANES : (c + 1) * LANES]
                    some = pl.ds(2 * pair + c, ORDER, stride=4)
                    if add:
                        z = z + dst[part, some, :]
                    dst[part, some, :] = z

    def middle(g, y):
        return swap_blocks(left(gate(g), swap_blocks(y)))

    halves = [(0, quarter, 2 * quarter, 3 * quarter)]
    gate(0)
    gate(1)
    for a in range(QUARTERS):
        load_x(a).wait()
    for half in range(1):
        first = 0
        x = jnp.concatenate([x_ref[pl.ds(2 * first + part, 4 * quarter, stride=2), :] for part in range(2)], 1)
        y = to_right(middle(1, to_left(right(gate(0), x))))
        store(sa, first, right(gate(4), y))
    strided(2, sa, sb)

    gate(3)
    gate(5)
    pl.semaphore_wait(barrier, nodes - 1)

    slot = reversed3(me & 7)
    part1 = rows // 8
    copies = []
    for orders in ((1, 0), (3, 2)):
        spots = [(slot >> 1) ^ order for order in orders]
        firsts = [pl.multiple_of(a * quarter, quarter) for a in spots]
        store_quarters(sc, firsts, middle(5, left(gate(3), load_quarters(sb, firsts))))
        for order, a, low in [(order, a, low) for order, a in zip(orders, spots) for low in (1, 0)]:
            if order == 0 and low == 0:
                mine = pl.ds(pl.multiple_of(slot * part1, part1), part1)
                r1[:, mine, :] = sc[:, mine, :]
                continue
            block = 2 * a + ((slot & 1) ^ low)
            index = 2 * order + low
            copy = pltpu.make_async_remote_copy(
                src_ref=sc.at[:, pl.ds(pl.multiple_of(block * part1, part1), part1), :],
                dst_ref=r1.at[:, pl.ds(pl.multiple_of(slot * part1, part1), part1), :],
                send_sem=send1.at[index],
                recv_sem=recv1.at[index],
                device_id={"node": (me & ~7) | reversed3(block)},
                device_id_type=pl.DeviceIdType.MESH,
            )
            copy.start()
            copies.append((index, copy))

    for g in (8, 7, 9):
        gate(g)
    halves_of(6, 0)

    arrivals = dict(copies)
    for near, group in enumerate(((0, 1, 2, 3), (4, 5, 6, 7))):
        firsts = []
        for index in group:
            if index in arrivals:
                arrivals[index].wait_recv()
            firsts.append(pl.multiple_of((slot ^ index) * part1, part1))
        x = jnp.concatenate(
            [
                jnp.concatenate([r1[part, pl.ds(first, part1), :] for part in range(2)], 1)
                for first in firsts
            ],
            0,
        )
        y = right(gate(8), x)
        for i, first in enumerate(firsts):
            store(sa, first, y[i * part1 : (i + 1) * part1])
        strided_half(0, sa, sb, (slot >> 2) ^ near, near == 1)

    part2 = rows // nodes
    per = nodes // QUARTERS
    early = part2 * LANES >= 1 << 11
    second = []
    mine = pl.ds(pl.multiple_of(me * part2, part2), part2)
    for orders in ((2,), (3,), (1, 0)):
        firsts = [pl.multiple_of(((me // per) ^ order) * quarter, quarter) for order in orders]
        y = left(gate(7), load_quarters(sb, firsts))
        if early:
            y = middle(9, y)
        store_quarters(sd, firsts, y)
        for order, low in [(order, low) for order in orders for low in range(per - 1, -1, -1)]:
            if order == 0 and low == 0:
                r2[:, mine, :] = sd[:, mine, :]
                continue
            block = me ^ (order * per + low)
            index = order * per + low
            copy = pltpu.make_async_remote_copy(
                src_ref=sd.at[:, pl.ds(pl.multiple_of(block * part2, part2), part2), :],
                dst_ref=r2.at[:, mine, :],
                send_sem=send2.at[index],
                recv_sem=recv2.at[index],
                device_id={"node": block},
                device_id_type=pl.DeviceIdType.MESH,
            )
            copy.start()
            second.append((index, copy))

    halves_of(10, 1)
    gate(11)
    for _, copy in copies:
        copy.wait_send()
    side = me // (nodes // 2)
    if early:
        for far in range(2):
            for index, copy in second:
                if index // (nodes // 2) == far:
                    copy.wait_recv()
            strided_half(1, r2, sa, side ^ far, far == 1)
    else:
        for _, copy in second:
            copy.wait_recv()
        for firsts in halves:
            store_quarters(sb, firsts, middle(9, load_quarters(r2, firsts)))
        for far in range(2):
            strided_half(1, sb, sa, side ^ far, far == 1)
    for firsts in halves:
        y = left(gate(11), load_quarters(sa, firsts))
        for i, first in enumerate(firsts):
            for part in range(2):
                o_ref[pl.ds(2 * first + part, quarter, stride=2), :] = y[
                    part * ORDER : (part + 1) * ORDER, i * LANES : (i + 1) * LANES
                ]
    for _, copy in second:
        copy.wait_send()


def body(nodes, amplitudes, gates):
    total = amplitudes.shape[1]
    distinct = gates.shape[1]
    rows = total // LANES
    x = amplitudes.reshape(2, rows, LANES).transpose(1, 0, 2).reshape(2 * rows, LANES)
    state = pltpu.VMEM((2, rows, LANES), F32)
    out = pl.pallas_call(
        functools.partial(kernel, nodes, distinct),
        out_shape=jax.ShapeDtypeStruct((2 * rows, LANES), F32),
        in_specs=[pl.BlockSpec(memory_space=pltpu.HBM)] * 2,
        out_specs=pl.BlockSpec(memory_space=pltpu.VMEM),
        scratch_shapes=[
            pltpu.VMEM((2 * rows, LANES), F32),
            pltpu.VMEM(gates.shape, F32),
            pltpu.VMEM((distinct, 2 * ORDER, 6 * ORDER), BF16),
            pltpu.VMEM((2, 2, 2 * ORDER, 3 * ORDER), BF16),
            state,
            state,
            state,
            state,
            state,
            state,
            pltpu.SemaphoreType.DMA((QUARTERS,)),
            pltpu.SemaphoreType.DMA((distinct,)),
            pltpu.SemaphoreType.DMA((8,)),
            pltpu.SemaphoreType.DMA((8,)),
            pltpu.SemaphoreType.DMA((nodes,)),
            pltpu.SemaphoreType.DMA((nodes,)),
        ],
        compiler_params=pltpu.CompilerParams(collective_id=0, has_side_effects=True, vmem_limit_bytes=53 << 20),
        name="circuit",
    )(x, gates)
    return out.reshape(rows, 2, LANES).transpose(1, 0, 2).reshape(2, total)


def solution(mesh):
    spec = P(None, ("paths", "node"))
    return jax.shard_map(
        functools.partial(body, mesh.shape["node"]), mesh=mesh, in_specs=(spec, P()), out_specs=spec, check_vma=False
    )
```

profile of v0, /device:TPU:13, one launch (start us, length us, event | category | flops | bytes accessed | tf_op | source)
XLA Modules:
  0.0 30.7 jit_solution(14802005220792051680)
XLA Ops:
  0.0 29.9 %circuit.1 = f32[1024,128]{1,0:T(8,128)S(1)} custom-call(f32[1024,128]{1,0:T(8,128)} %bitcast.11, f32[2,12,128,128]{3,2,1,0:T(8,128)} %g_hbm.1), custom_call_target="tpu_custom_call" | custom-call | tf_op jit(solution)/shard_map/circuit/pallas_call | solution.py:347
  29.9 0.8 %copy.6 = f32[2,65536]{1,0:T(2,128)} copy(f32[2,65536]{1,0:T(2,128)S(1)} %bitcast.10) | data formatting | bytes 1048576
where the time goes:
time: 30.9 us; the launch traced here: 30.7 us
  Pallas kernels  29.9 us (97%)
  local copies, waits for them, and re-layouts  0.8 us (3%)
    pallas_call x1, Pallas kernels, body(): pl.pallas_call(functools.partial(kernel, nodes, distinct), out_shape=jax....  29.9 us
    unnamed x1, local copies, waits for them, and re-layouts  0.8 us

commit v1 on v0

--- a/solution.py
+++ b/solution.py
@@ -126,11 +126,12 @@
     def load_gate(m):
         return pltpu.make_async_copy(g_hbm.at[:, m], g_ref.at[:, m], in_g.at[m])
 
-    sequence = list(dict.fromkeys(g % distinct for g in (0, 1, 4, 2, 3, 5, 8, 6, 7, 9, 10, 11)))
-    load_gate(sequence[0]).start()
+    sequence = list(dict.fromkeys(g % distinct for g in (0, 1, 2, 3, 4, 5, 8, 6, 7, 9, 10, 11)))
+    for m in sequence[:2]:
+        load_gate(m).start()
     for a in range(QUARTERS):
         load_x(a).start()
-    for m in sequence[1:]:
+    for m in sequence[2:]:
         load_gate(m).start()
     me = lax.axis_index("node")
     barrier = pltpu.get_barrier_semaphore()
@@ -217,20 +218,20 @@
     def middle(g, y):
         return swap_blocks(left(gate(g), swap_blocks(y)))
 
+    def low_gates(x):
+        y = to_right(middle(5, to_left(right(gate(4), x))))
+        return right(gate(8), y)
+
     halves = [(0, quarter, 2 * quarter, 3 * quarter)]
     gate(0)
     gate(1)
     for a in range(QUARTERS):
         load_x(a).wait()
-    for half in range(1):
-        first = 0
-        x = jnp.concatenate([x_ref[pl.ds(2 * first + part, 4 * quarter, stride=2), :] for part in range(2)], 1)
-        y = to_right(middle(1, to_left(right(gate(0), x))))
-        store(sa, first, right(gate(4), y))
+    x = jnp.concatenate([x_ref[pl.ds(part, rows, stride=2), :] for part in range(2)], 1)
+    store(sa, 0, to_right(middle(1, to_left(right(gate(0), x)))))
+    gate(2)
+    gate(3)
     strided(2, sa, sb)
-
-    gate(3)
-    gate(5)
     pl.semaphore_wait(barrier, nodes - 1)
 
     slot = reversed3(me & 7)
@@ -239,7 +240,13 @@
     for orders in ((1, 0), (3, 2)):
         spots = [(slot >> 1) ^ order for order in orders]
         firsts = [pl.multiple_of(a * quarter, quarter) for a in spots]
-        store_quarters(sc, firsts, middle(5, left(gate(3), load_quarters(sb, firsts))))
+        y = left(gate(3), load_quarters(sb, firsts))
+        if 0 in orders:
+            store_quarters(sc, firsts, y)
+        else:
+            y = low_gates(to_right(y))
+            for i, first in enumerate(firsts):
+                store(sc, first, y[i * quarter : (i + 1) * quarter])
         for order, a, low in [(order, a, low) for order, a in zip(orders, spots) for low in (1, 0)]:
             if order == 0 and low == 0:
                 mine = pl.ds(pl.multiple_of(slot * part1, part1), part1)
@@ -258,28 +265,26 @@
             copy.start()
             copies.append((index, copy))
 
-    for g in (8, 7, 9):
-        gate(g)
     halves_of(6, 0)
+    gate(7)
+    gate(9)
 
     arrivals = dict(copies)
-    for near, group in enumerate(((0, 1, 2, 3), (4, 5, 6, 7))):
-        firsts = []
-        for index in group:
-            if index in arrivals:
-                arrivals[index].wait_recv()
-            firsts.append(pl.multiple_of((slot ^ index) * part1, part1))
-        x = jnp.concatenate(
-            [
-                jnp.concatenate([r1[part, pl.ds(first, part1), :] for part in range(2)], 1)
-                for first in firsts
-            ],
-            0,
-        )
-        y = right(gate(8), x)
-        for i, first in enumerate(firsts):
-            store(sa, first, y[i * part1 : (i + 1) * part1])
-        strided_half(0, sa, sb, (slot >> 2) ^ near, near == 1)
+    firsts = []
+    for index in range(4):
+        if index in arrivals:
+            arrivals[index].wait_recv()
+        firsts.append(pl.multiple_of((slot ^ index) * part1, part1))
+    x = jnp.concatenate(
+        [jnp.concatenate([r1[part, pl.ds(first, part1), :] for part in range(2)], 1) for first in firsts], 0
+    )
+    y = low_gates(x)
+    for i, first in enumerate(firsts):
+        store(sa, first, y[i * part1 : (i + 1) * part1])
+    strided_half(0, sa, sb, slot >> 2, False)
+    for index in range(4, 8):
+        arrivals[index].wait_recv()
+    strided_half(0, r1, sb, (slot >> 2) ^ 1, True)
 
     part2 = rows // nodes
     per = nodes // QUARTERS

time: 30.9 us -> 29.1 us (0.942); the launches traced: 30.7 us -> 28.5 us
  Pallas kernels: 29.9 us -> 27.7 us
    pallas_call x1, Pallas kernels: 29.9 us -> 27.7 us  [body(): pl.pallas_call(functools.partial(kernel, nodes, distinct), out_shape=jax....]
where the time goes in v1:
time: 29.1 us; the launch traced here: 28.5 us
  Pallas kernels  27.7 us (95%)
  local copies, waits for them, and re-layouts  0.8 us (3%)
    pallas_call x1, Pallas kernels, body(): pl.pallas_call(functools.partial(kernel, nodes, distinct), out_shape=jax....  27.7 us
    unnamed x1, local copies, waits for them, and re-layouts  0.8 us

profile of v1, /device:TPU:13, one launch (start us, length us, event | category | flops | bytes accessed | tf_op | source)
XLA Modules:
  0.0 28.5 jit_solution(3288396696275683291)
XLA Ops:
  0.0 27.7 %circuit.1 = f32[1024,128]{1,0:T(8,128)S(1)} custom-call(f32[1024,128]{1,0:T(8,128)} %bitcast.11, f32[2,12,128,128]{3,2,1,0:T(8,128)} %g_hbm.1), custom_call_target="tpu_custom_call" | custom-call | tf_op jit(solution)/shard_map/circuit/pallas_call | solution.py:352
  27.7 0.8 %copy.6 = f32[2,65536]{1,0:T(2,128)} copy(f32[2,65536]{1,0:T(2,128)S(1)} %bitcast.10) | data formatting | bytes 1048576

commit v2 on v1

--- a/solution.py
+++ b/solution.py
@@ -237,11 +237,11 @@
     slot = reversed3(me & 7)
     part1 = rows // 8
     copies = []
-    for orders in ((1, 0), (3, 2)):
+    for orders in ((1,), (0,), (3, 2)):
         spots = [(slot >> 1) ^ order for order in orders]
         firsts = [pl.multiple_of(a * quarter, quarter) for a in spots]
         y = left(gate(3), load_quarters(sb, firsts))
-        if 0 in orders:
+        if max(orders) < 2:
             store_quarters(sc, firsts, y)
         else:
             y = low_gates(to_right(y))
@@ -291,7 +291,7 @@
     early = part2 * LANES >= 1 << 11
     second = []
     mine = pl.ds(pl.multiple_of(me * part2, part2), part2)
-    for orders in ((2,), (3,), (1, 0)):
+    for orders in ((2,), (3, 1), (0,)):
         firsts = [pl.multiple_of(((me // per) ^ order) * quarter, quarter) for order in orders]
         y = left(gate(7), load_quarters(sb, firsts))
         if early:

time: 29.1 us -> 28.5 us (0.979); the launches traced: 28.5 us -> 28.4 us
  no operation moved by 1% of the time
where the time goes in v2:
time: 28.5 us; the launch traced here: 28.4 us
  Pallas kernels  27.6 us (97%)
  local copies, waits for them, and re-layouts  0.8 us (3%)
    pallas_call x1, Pallas kernels, body(): pl.pallas_call(functools.partial(kernel, nodes, distinct), out_shape=jax....  27.6 us
    unnamed x1, local copies, waits for them, and re-layouts  0.8 us

profile of v2, /device:TPU:13, one launch (start us, length us, event | category | flops | bytes accessed | tf_op | source)
XLA Modules:
  0.0 28.4 jit_solution(17834806442908410352)
XLA Ops:
  0.0 27.6 %circuit.1 = f32[1024,128]{1,0:T(8,128)S(1)} custom-call(f32[1024,128]{1,0:T(8,128)} %bitcast.11, f32[2,12,128,128]{3,2,1,0:T(8,128)} %g_hbm.1), custom_call_target="tpu_custom_call" | custom-call | tf_op jit(solution)/shard_map/circuit/pallas_call | solution.py:352
  27.6 0.8 %copy.6 = f32[2,65536]{1,0:T(2,128)} copy(f32[2,65536]{1,0:T(2,128)S(1)} %bitcast.10) | data formatting | bytes 1048576

commit v3 on v2

--- a/solution.py
+++ b/solution.py
@@ -289,45 +289,61 @@
     part2 = rows // nodes
     per = nodes // QUARTERS
     early = part2 * LANES >= 1 << 11
-    second = []
     mine = pl.ds(pl.multiple_of(me * part2, part2), part2)
-    for orders in ((2,), (3, 1), (0,)):
-        firsts = [pl.multiple_of(((me // per) ^ order) * quarter, quarter) for order in orders]
+    spot = me // per
+    even = 1 - (spot & 1)
+    side = me // (nodes // 2)
+
+    def second(index):
+        block = me ^ index
+        return pltpu.make_async_remote_copy(
+            src_ref=sd.at[:, pl.ds(pl.multiple_of(block * part2, part2), part2), :],
+            dst_ref=r2.at[:, mine, :],
+            send_sem=send2.at[index],
+            recv_sem=recv2.at[index],
+            device_id={"node": block},
+            device_id_type=pl.DeviceIdType.MESH,
+        )
+
+    for phase, orders in enumerate(((3 - even,), (1, 2 + even), (0,))):
+        firsts = [pl.multiple_of((spot ^ order) * quarter, quarter) for order in orders]
         y = left(gate(7), load_quarters(sb, firsts))
-        if early:
+        if early and phase > 0:
             y = middle(9, y)
         store_quarters(sd, firsts, y)
         for order, low in [(order, low) for order in orders for low in range(per - 1, -1, -1)]:
-            if order == 0 and low == 0:
+            if isinstance(order, int) and order == 0 and low == 0:
                 r2[:, mine, :] = sd[:, mine, :]
-                continue
-            block = me ^ (order * per + low)
-            index = order * per + low
-            copy = pltpu.make_async_remote_copy(
-                src_ref=sd.at[:, pl.ds(pl.multiple_of(block * part2, part2), part2), :],
-                dst_ref=r2.at[:, mine, :],
-                send_sem=send2.at[index],
-                recv_sem=recv2.at[index],
-                device_id={"node": block},
-                device_id_type=pl.DeviceIdType.MESH,
-            )
-            copy.start()
-            second.append((index, copy))
+            else:
+                second(order * per + low).start()
 
     halves_of(10, 1)
     gate(11)
     for _, copy in copies:
         copy.wait_send()
-    side = me // (nodes // 2)
     if early:
-        for far in range(2):
-            for index, copy in second:
-                if index // (nodes // 2) == far:
-                    copy.wait_recv()
-            strided_half(1, r2, sa, side ^ far, far == 1)
+
+        def arrive_half(far):
+            for low in range(1, nodes // 2):
+                second(far * (nodes // 2) + low).wait_recv()
+
+            @pl.when(far == 1)
+            def _():
+                second(nodes // 2).wait_recv()
+
+        arrive_half(even)
+
+        @pl.when(even == 1)
+        def _():
+            firsts = [pl.multiple_of((spot ^ order) * quarter, quarter) for order in (2, 3)]
+            store_quarters(r2, firsts, middle(9, load_quarters(r2, firsts)))
+
+        strided_half(1, r2, sa, side ^ even, False)
+        arrive_half(1 - even)
+        strided_half(1, r2, sa, side ^ (1 - even), True)
     else:
-        for _, copy in second:
-            copy.wait_recv()
+        for index in range(1, nodes):
+            second(index).wait_recv()
         for firsts in halves:
             store_quarters(sb, firsts, middle(9, load_quarters(r2, firsts)))
         for far in range(2):
@@ -339,8 +355,8 @@
                 o_ref[pl.ds(2 * first + part, quarter, stride=2), :] = y[
                     part * ORDER : (part + 1) * ORDER, i * LANES : (i + 1) * LANES
                 ]
-    for _, copy in second:
-        copy.wait_send()
+    for index in range(1, nodes):
+        second(index).wait_send()
 
 
 def body(nodes, amplitudes, gates):

time: 28.5 us -> 28.1 us (0.986)
  Pallas kernels: 27.6 us -> 27.1 us
    pallas_call x1, Pallas kernels: 27.6 us -> 27.1 us  [body(): pl.pallas_call(functools.partial(kernel, nodes, distinct), out_shape=jax....]
where the time goes in v3:
time: 28.1 us; the launch traced here: 27.9 us
  Pallas kernels  27.1 us (96%)
  local copies, waits for them, and re-layouts  0.8 us (3%)
    pallas_call x1, Pallas kernels, body(): pl.pallas_call(functools.partial(kernel, nodes, distinct), out_shape=jax....  27.1 us
    unnamed x1, local copies, waits for them, and re-layouts  0.8 us

profile of v3, /device:TPU:13, one launch (start us, length us, event | category | flops | bytes accessed | tf_op | source)
XLA Modules:
  0.0 27.9 jit_solution(11502206342975981736)
XLA Ops:
  0.0 27.1 %circuit.1 = f32[1024,128]{1,0:T(8,128)S(1)} custom-call(f32[1024,128]{1,0:T(8,128)} %bitcast.11, f32[2,12,128,128]{3,2,1,0:T(8,128)} %g_hbm.1), custom_call_target="tpu_custom_call" | custom-call | tf_op jit(solution)/shard_map/circuit/pallas_call | solution.py:368
  27.1 0.8 %copy.6 = f32[2,65536]{1,0:T(2,128)} copy(f32[2,65536]{1,0:T(2,128)S(1)} %bitcast.10) | data formatting | bytes 1048576

commit v4 on v3

--- a/solution.py
+++ b/solution.py
@@ -12,6 +12,7 @@
 ORDER = 128
 LANES = 128
 QUARTERS = 4
+GROUPS = (0, 2, 4, 6)
 
 
 def split(x):
@@ -119,20 +120,17 @@
     rows = sa.shape[1]
     quarter = rows // QUARTERS
 
-    def load_x(a):
-        some = pl.ds(2 * a * quarter, 2 * quarter)
-        return pltpu.make_async_copy(x_hbm.at[some, :], x_ref.at[some, :], in_x.at[a])
-
-    def load_gate(m):
-        return pltpu.make_async_copy(g_hbm.at[:, m], g_ref.at[:, m], in_g.at[m])
-
-    sequence = list(dict.fromkeys(g % distinct for g in (0, 1, 2, 3, 4, 5, 8, 6, 7, 9, 10, 11)))
-    for m in sequence[:2]:
-        load_gate(m).start()
-    for a in range(QUARTERS):
-        load_x(a).start()
-    for m in sequence[2:]:
-        load_gate(m).start()
+    load_x = pltpu.make_async_copy(x_hbm, x_ref, in_x.at[0])
+    bounds = (*GROUPS, distinct)
+
+    def load_gates(i):
+        some = pl.ds(bounds[i], bounds[i + 1] - bounds[i])
+        return pltpu.make_async_copy(g_hbm.at[:, some], g_ref.at[:, some], in_g.at[i])
+
+    load_gates(0).start()
+    load_x.start()
+    for i in range(1, len(GROUPS)):
+        load_gates(i).start()
     me = lax.axis_index("node")
     barrier = pltpu.get_barrier_semaphore()
     for i in range(1, nodes):
@@ -142,9 +140,10 @@
     loaded = set()
 
     def arrive(m):
-        if m not in loaded:
-            loaded.add(m)
-            load_gate(m).wait()
+        i = sum(m >= bound for bound in GROUPS) - 1
+        if i not in loaded:
+            loaded.add(i)
+            load_gates(i).wait()
 
     def gate(g):
         m = g % distinct
@@ -188,6 +187,9 @@
                     dst[part, pl.ds(2 * pair + c, ORDER, stride=4), :] = y[
                         part * ORDER : (part + 1) * ORDER, c * LANES : (c + 1) * LANES
                     ]
+
+    def finish(ref, some, sem):
+        pltpu.make_async_copy(ref.at[:, pl.ds(0, some), :], ref.at[:, pl.ds(0, some), :], sem).wait()
 
     def halves_of(g, k):
         arrive(g % distinct)
@@ -225,8 +227,7 @@
     halves = [(0, quarter, 2 * quarter, 3 * quarter)]
     gate(0)
     gate(1)
-    for a in range(QUARTERS):
-        load_x(a).wait()
+    load_x.wait()
     x = jnp.concatenate([x_ref[pl.ds(part, rows, stride=2), :] for part in range(2)], 1)
     store(sa, 0, to_right(middle(1, to_left(right(gate(0), x)))))
     gate(2)
@@ -236,7 +237,6 @@
 
     slot = reversed3(me & 7)
     part1 = rows // 8
-    copies = []
     for orders in ((1,), (0,), (3, 2)):
         spots = [(slot >> 1) ^ order for order in orders]
         firsts = [pl.multiple_of(a * quarter, quarter) for a in spots]
@@ -254,27 +254,21 @@
                 continue
             block = 2 * a + ((slot & 1) ^ low)
             index = 2 * order + low
-            copy = pltpu.make_async_remote_copy(
+            pltpu.make_async_remote_copy(
                 src_ref=sc.at[:, pl.ds(pl.multiple_of(block * part1, part1), part1), :],
                 dst_ref=r1.at[:, pl.ds(pl.multiple_of(slot * part1, part1), part1), :],
-                send_sem=send1.at[index],
-                recv_sem=recv1.at[index],
+                send_sem=send1.at[0],
+                recv_sem=recv1.at[index // 4],
                 device_id={"node": (me & ~7) | reversed3(block)},
                 device_id_type=pl.DeviceIdType.MESH,
-            )
-            copy.start()
-            copies.append((index, copy))
+            ).start()
 
     halves_of(6, 0)
     gate(7)
     gate(9)
 
-    arrivals = dict(copies)
-    firsts = []
-    for index in range(4):
-        if index in arrivals:
-            arrivals[index].wait_recv()
-        firsts.append(pl.multiple_of((slot ^ index) * part1, part1))
+    finish(r1, 3 * part1, recv1.at[0])
+    firsts = [pl.multiple_of((slot ^ index) * part1, part1) for index in range(4)]
     x = jnp.concatenate(
         [jnp.concatenate([r1[part, pl.ds(first, part1), :] for part in range(2)], 1) for first in firsts], 0
     )
@@ -282,8 +276,7 @@
     for i, first in enumerate(firsts):
         store(sa, first, y[i * part1 : (i + 1) * part1])
     strided_half(0, sa, sb, slot >> 2, False)
-    for index in range(4, 8):
-        arrivals[index].wait_recv()
+    finish(r1, 4 * part1, recv1.at[1])
     strided_half(0, r1, sb, (slot >> 2) ^ 1, True)
 
     part2 = rows // nodes
@@ -294,13 +287,13 @@
     even = 1 - (spot & 1)
     side = me // (nodes // 2)
 
-    def second(index):
+    def second(index, far):
         block = me ^ index
         return pltpu.make_async_remote_copy(
             src_ref=sd.at[:, pl.ds(pl.multiple_of(block * part2, part2), part2), :],
             dst_ref=r2.at[:, mine, :],
-            send_sem=send2.at[index],
-            recv_sem=recv2.at[index],
+            send_sem=send2.at[0],
+            recv_sem=recv2.at[far],
             device_id={"node": block},
             device_id_type=pl.DeviceIdType.MESH,
         )
@@ -315,35 +308,41 @@
             if isinstance(order, int) and order == 0 and low == 0:
                 r2[:, mine, :] = sd[:, mine, :]
             else:
-                second(order * per + low).start()
+                second(order * per + low, 0 if isinstance(order, int) and order < 2 else 1).start()
 
     halves_of(10, 1)
     gate(11)
-    for _, copy in copies:
-        copy.wait_send()
+    finish(sc, 7 * part1, send1.at[0])
+
+    def arrive_half(far):
+        finish(r2, (nodes // 2 - 1 + far) * part2, recv2.at[far])
+
     if early:
 
-        def arrive_half(far):
-            for low in range(1, nodes // 2):
-                second(far * (nodes // 2) + low).wait_recv()
-
-            @pl.when(far == 1)
-            def _():
-                second(nodes // 2).wait_recv()
-
-        arrive_half(even)
+        @pl.when(even == 0)
+        def _():
+            arrive_half(0)
 
         @pl.when(even == 1)
         def _():
+            arrive_half(1)
             firsts = [pl.multiple_of((spot ^ order) * quarter, quarter) for order in (2, 3)]
             store_quarters(r2, firsts, middle(9, load_quarters(r2, firsts)))
 
         strided_half(1, r2, sa, side ^ even, False)
-        arrive_half(1 - even)
+
+        @pl.when(even == 0)
+        def _():
+            arrive_half(1)
+
+        @pl.when(even == 1)
+        def _():
+            arrive_half(0)
+
         strided_half(1, r2, sa, side ^ (1 - even), True)
     else:
-        for index in range(1, nodes):
-            second(index).wait_recv()
+        arrive_half(0)
+        arrive_half(1)
         for firsts in halves:
             store_quarters(sb, firsts, middle(9, load_quarters(r2, firsts)))
         for far in range(2):
@@ -355,8 +354,7 @@
                 o_ref[pl.ds(2 * first + part, quarter, stride=2), :] = y[
                     part * ORDER : (part + 1) * ORDER, i * LANES : (i + 1) * LANES
                 ]
-    for index in range(1, nodes):
-        second(index).wait_send()
+    finish(sd, (nodes - 1) * part2, send2.at[0])
 
 
 def body(nodes, amplitudes, gates):
@@ -381,12 +379,12 @@
             state,
             state,
             state,
-            pltpu.SemaphoreType.DMA((QUARTERS,)),
-            pltpu.SemaphoreType.DMA((distinct,)),
-            pltpu.SemaphoreType.DMA((8,)),
-            pltpu.SemaphoreType.DMA((8,)),
-            pltpu.SemaphoreType.DMA((nodes,)),
-            pltpu.SemaphoreType.DMA((nodes,)),
+            pltpu.SemaphoreType.DMA((1,)),
+            pltpu.SemaphoreType.DMA((len(GROUPS),)),
+            pltpu.SemaphoreType.DMA((1,)),
+            pltpu.SemaphoreType.DMA((2,)),
+            pltpu.SemaphoreType.DMA((1,)),
+            pltpu.SemaphoreType.DMA((2,)),
         ],
         compiler_params=pltpu.CompilerParams(collective_id=0, has_side_effects=True, vmem_limit_bytes=53 << 20),
         name="circuit",

time: 28.1 us -> 27.4 us (0.975)
  Pallas kernels: 27.1 us -> 26.4 us
    pallas_call x1, Pallas kernels: 27.1 us -> 26.4 us  [body(): pl.pallas_call(functools.partial(kernel, nodes, distinct), out_shape=jax....]
where the time goes in v4:
time: 27.4 us; the launch traced here: 27.2 us
  Pallas kernels  26.4 us (96%)
  local copies, waits for them, and re-layouts  0.8 us (3%)
    pallas_call x1, Pallas kernels, body(): pl.pallas_call(functools.partial(kernel, nodes, distinct), out_shape=jax....  26.4 us
    unnamed x1, local copies, waits for them, and re-layouts  0.8 us

profile of v4, /device:TPU:13, one launch (start us, length us, event | category | flops | bytes accessed | tf_op | source)
XLA Modules:
  0.0 27.2 jit_solution(12173003035749119390)
XLA Ops:
  0.0 26.4 %circuit.1 = f32[1024,128]{1,0:T(8,128)S(1)} custom-call(f32[1024,128]{1,0:T(8,128)} %bitcast.11, f32[2,12,128,128]{3,2,1,0:T(8,128)} %g_hbm.1), custom_call_target="tpu_custom_call" | custom-call | tf_op jit(solution)/shard_map/circuit/pallas_call | solution.py:366
  26.4 0.8 %copy.6 = f32[2,65536]{1,0:T(2,128)} copy(f32[2,65536]{1,0:T(2,128)S(1)} %bitcast.10) | data formatting | bytes 1048576

commit v5 on v4

--- a/solution.py
+++ b/solution.py
@@ -104,6 +104,11 @@
 
 
 def right(gate, x):
+    some = x.shape[0] // 2
+    return jnp.concatenate([right_rows(gate, x[:some]), right_rows(gate, x[some:])], 0)
+
+
+def right_rows(gate, x):
     high, low = split(x)
     return lax.dot_general(
         jnp.concatenate([high, high, low], 1), gate, (((1,), (1,)), ((), ())), preferred_element_type=F32
@@ -233,7 +238,6 @@
     gate(2)
     gate(3)
     strided(2, sa, sb)
-    pl.semaphore_wait(barrier, nodes - 1)
 
     slot = reversed3(me & 7)
     part1 = rows // 8
@@ -247,6 +251,8 @@
             y = low_gates(to_right(y))
             for i, first in enumerate(firsts):
                 store(sc, first, y[i * quarter : (i + 1) * quarter])
+        if 1 in orders:
+            pl.semaphore_wait(barrier, nodes - 1)
         for order, a, low in [(order, a, low) for order, a in zip(orders, spots) for low in (1, 0)]:
             if order == 0 and low == 0:
                 mine = pl.ds(pl.multiple_of(slot * part1, part1), part1)

time: 27.4 us -> 27.1 us (0.989)
  no operation moved by 1% of the time
where the time goes in v5:
time: 27.1 us; the launch traced here: 27 us
  Pallas kernels  26.2 us (97%)
  local copies, waits for them, and re-layouts  0.8 us (3%)
    pallas_call x1, Pallas kernels, body(): pl.pallas_call(functools.partial(kernel, nodes, distinct), out_shape=jax....  26.2 us
    unnamed x1, local copies, waits for them, and re-layouts  0.8 us

profile of v5, /device:TPU:13, one launch (start us, length us, event | category | flops | bytes accessed | tf_op | source)
XLA Modules:
  0.0 27.0 jit_solution(12586590043015244575)
XLA Ops:
  0.0 26.2 %circuit.1 = f32[1024,128]{1,0:T(8,128)S(1)} custom-call(f32[1024,128]{1,0:T(8,128)} %bitcast.11, f32[2,12,128,128]{3,2,1,0:T(8,128)} %g_hbm.1), custom_call_target="tpu_custom_call" | custom-call | tf_op jit(solution)/shard_map/circuit/pallas_call | solution.py:372
  26.2 0.8 %copy.6 = f32[2,65536]{1,0:T(2,128)} copy(f32[2,65536]{1,0:T(2,128)S(1)} %bitcast.10) | data formatting | bytes 1048576
